TPU v7x, 32 devices: a whole 2x2x4 slice. The times are simulated.
32 devices in a mesh: row: 2 (over y), col: 16 (over z, x, core).
Axes of the slice: x: 2, y: 2, z: 4, core: 2. Of those that a mesh axis runs over, the one named last changes fastest.
Arguments:
- coefficients: float32 [2, 2, 8, 2048, 512], P(None, None, None, ('row', 'col')), may hold values from -6 to 6
- vertical_modes: float32 [512, 512], replicated, may hold values from -0.25 to 0.25
- mode_slopes: float32 [512, 512], replicated, may hold values from -0.25 to 0.25
- dual_modes: float32 [512, 512], replicated, may hold values from -0.25 to 0.25
- eigenvalues: float32 [512], replicated, may hold values from 0.01 to 10
- velocity: float32 [3, 512, 2048], P(None, 'col'), may hold values from -5 to 5
- gradient: float32 [2, 512], P(None, 'col'), may hold values from 0.2 to 2
- span_wavenumbers: float32 [8], replicated, may hold values from 0 to 2
- implicit_rates: float32 [2], replicated, may hold values from 0.02 to 0.2
- time_step: float32 [], replicated, may hold values from 0.2 to 0.5
Outputs:
- new_coefficients: float32 [2, 2, 8, 2048, 512], P(None, None, None, ('row', 'col'))
All inputs are finite; a program needn't handle non-finite values.
Results may differ from a plain program's by a relative error of at most 0.00005.
Values sent between devices are 32-bit elements; how exact they have to be, the bound alone decides.
A program may use at most 128 MiB of HBM per device.

v0:
```python
import math

import jax
import jax.numpy as jnp
from jax import lax
from jax.sharding import PartitionSpec as P

highest = lax.Precision.HIGHEST
lane_width = 128


def signed_waves(length):
    indices = jnp.arange(length, dtype=jnp.int32)
    return jnp.where(indices < length // 2, indices, indices - length)


def phase_table(row_total, col_total, period, direction):
    left_index = jnp.arange(row_total, dtype=jnp.int32)[:, None]
    right_index = jnp.arange(col_total, dtype=jnp.int32)[None, :]
    angles = (left_index * right_index % period).astype(jnp.float32) * (2.0 * math.pi / period)
    return (jnp.cos(angles), direction * jnp.sin(angles))


def contract(form, left_real, left_imag, right_real, right_imag):
    product_real = jnp.einsum(form, left_real, right_real, precision=highest) - jnp.einsum(
        form, left_imag, right_imag, precision=highest
    )
    product_imag = jnp.einsum(form, left_real, right_imag, precision=highest) + jnp.einsum(
        form, left_imag, right_real, precision=highest
    )
    return (product_real, product_imag)


def twisted(real_in, imag_in, twist_real, twist_imag):
    return (
        real_in * twist_real - imag_in * twist_imag,
        real_in * twist_imag + imag_in * twist_real,
    )


def inverse_transform(real_in, imag_in, length):
    short_size = length // lane_width
    scale = 1.0 / math.sqrt(length)
    short_real, short_imag = phase_table(short_size, short_size, short_size, 1.0)
    twist_real, twist_imag = phase_table(short_size, lane_width, length, 1.0)
    wide_real, wide_imag = phase_table(lane_width, lane_width, lane_width, 1.0)
    middle_real, middle_imag = contract("...ef,ed->...df", real_in, imag_in, short_real, short_imag)
    middle_real, middle_imag = twisted(middle_real, middle_imag, twist_real, twist_imag)
    return contract(
        "...df,fc->...dc", middle_real, middle_imag, wide_real * scale, wide_imag * scale
    )


def forward_transform(real_in, imag_in, length):
    short_size = length // lane_width
    scale = 1.0 / math.sqrt(length)
    short_real, short_imag = phase_table(short_size, short_size, short_size, -1.0)
    twist_real, twist_imag = phase_table(short_size, lane_width, length, -1.0)
    wide_real, wide_imag = phase_table(lane_width, lane_width, lane_width, -1.0)
    middle_real, middle_imag = contract("...dc,cf->...df", real_in, imag_in, wide_real, wide_imag)
    middle_real, middle_imag = twisted(middle_real, middle_imag, twist_real, twist_imag)
    return contract(
        "...df,de->...ef", middle_real, middle_imag, short_real * scale, short_imag * scale
    )


def on_device(
    coefficients,
    vertical_modes,
    mode_slopes,
    dual_modes,
    eigenvalues,
    velocity,
    gradient,
    span_wavenumbers,
    implicit_rates,
    time_step,
):
    row_count = lax.axis_size("row")
    col_count = lax.axis_size("col")
    local_waves = coefficients.shape[3]
    total_points = local_waves * row_count * col_count
    short_size = total_points // lane_width
    first_wave = (lax.axis_index("row") * col_count + lax.axis_index("col")) * local_waves
    signed = signed_waves(total_points)
    zonal_waves = signed.astype(jnp.float32) * (2.0 * math.pi / total_points)
    own_waves = lax.dynamic_slice_in_dim(zonal_waves, first_wave, local_waves)
    value_real = jnp.einsum("sqpj,zj->zsqp", coefficients[:, 0], vertical_modes, precision=highest)
    value_imag = jnp.einsum("sqpj,zj->zsqp", coefficients[:, 1], vertical_modes, precision=highest)
    slope_real = jnp.einsum("sqpj,zj->zsqp", coefficients[:, 0], mode_slopes, precision=highest)
    slope_imag = jnp.einsum("sqpj,zj->zsqp", coefficients[:, 1], mode_slopes, precision=highest)
    fields = (
        lax.all_to_all(value_real, "col", split_axis=0, concat_axis=3, tiled=True),
        lax.all_to_all(value_imag, "col", split_axis=0, concat_axis=3, tiled=True),
        lax.all_to_all(slope_real, "col", split_axis=0, concat_axis=3, tiled=True),
        lax.all_to_all(slope_imag, "col", split_axis=0, concat_axis=3, tiled=True),
    )
    fields = (
        lax.all_to_all(fields[0], "row", split_axis=2, concat_axis=3, tiled=True),
        lax.all_to_all(fields[1], "row", split_axis=2, concat_axis=3, tiled=True),
        lax.all_to_all(fields[2], "row", split_axis=2, concat_axis=3, tiled=True),
        lax.all_to_all(fields[3], "row", split_axis=2, concat_axis=3, tiled=True),
    )
    level_rows = fields[0].shape[0]
    span_rows = fields[0].shape[2]
    grid_shape = (level_rows, 2, span_rows, short_size, lane_width)
    value_real = fields[0].reshape(grid_shape)
    value_imag = fields[1].reshape(grid_shape)
    slope_real = fields[2].reshape(grid_shape)
    slope_imag = fields[3].reshape(grid_shape)
    wave_grid = zonal_waves.reshape(short_size, lane_width)
    scalar_real, scalar_imag = inverse_transform(value_real, value_imag, total_points)
    zonal_real, zonal_imag = inverse_transform(
        -wave_grid * value_imag, wave_grid * value_real, total_points
    )
    rise_real, rise_imag = inverse_transform(slope_real, slope_imag, total_points)
    flow = jnp.swapaxes(velocity.reshape(3, level_rows, lane_width, short_size), -1, -2)
    zonal_flow = flow[0][:, None, None]
    span_flow = flow[1][:, None, None]
    rise_flow = flow[2][:, None, None]
    span_waves = lax.dynamic_slice_in_dim(
        span_wavenumbers, lax.axis_index("row") * span_rows, span_rows
    )[None, None, :, None, None]
    background = jnp.transpose(gradient)[:, :, None, None, None]
    advect_real = (
        zonal_flow * zonal_real
        - span_waves * span_flow * scalar_imag
        + rise_flow * rise_real
        + rise_flow * background
    )
    advect_imag = (
        zonal_flow * zonal_imag + span_waves * span_flow * scalar_real + rise_flow * rise_imag
    )
    spectra_real, spectra_imag = forward_transform(advect_real, advect_imag, total_points)
    retained = (
        (jnp.abs(signed) <= total_points // 3).astype(jnp.float32).reshape(short_size, lane_width)
    )
    flat_shape = (level_rows, 2, span_rows, total_points)
    spectra_real = (spectra_real * retained).reshape(flat_shape)
    spectra_imag = (spectra_imag * retained).reshape(flat_shape)
    returned_real, returned_imag = (
        lax.all_to_all(
            lax.all_to_all(spectra_real, "row", split_axis=3, concat_axis=2, tiled=True),
            "col",
            split_axis=3,
            concat_axis=0,
            tiled=True,
        ),
        lax.all_to_all(
            lax.all_to_all(spectra_imag, "row", split_axis=3, concat_axis=2, tiled=True),
            "col",
            split_axis=3,
            concat_axis=0,
            tiled=True,
        ),
    )
    forcing_real = jnp.einsum("zsqp,jz->sqpj", returned_real, dual_modes, precision=highest)
    forcing_imag = jnp.einsum("zsqp,jz->sqpj", returned_imag, dual_modes, precision=highest)
    forcing = jnp.stack([forcing_real, forcing_imag], 1)
    denominator = 1.0 + implicit_rates[:, None, None, None, None] * (
        eigenvalues[None, None, None, None, :]
        + own_waves[None, None, None, :, None] ** 2
        + span_wavenumbers[None, None, :, None, None] ** 2
    )
    return (coefficients - time_step * forcing) / denominator


def solution(mesh):
    in_specs = (
        P(None, None, None, ("row", "col"), None),
        P(),
        P(),
        P(),
        P(),
        P(None, "col", None),
        P(None, "col"),
        P(),
        P(),
        P(),
    )
    out_specs = P(None, None, None, ("row", "col"), None)
    return jax.shard_map(
        on_device, mesh=mesh, in_specs=in_specs, out_specs=out_specs, check_vma=False
    )
```

profile of v0, /device:TPU:15, one launch (start us, length us, event | category | flops | bytes accessed | tf_op | source)
XLA Modules:
  0.0 696.3 jit_solution(4996307598044424374)
XLA Ops:
  36.5 33.1 %all-to-all-done.2 = f32[16,1,32768]{2,1,0:T(1,128)} async-done(((f32[16,1,32768]{2,1,0:T(1,128)}), f32[16,1,32768]{2,1,0:T(1,128)}, u32[]{:S(2)}, u32[]{:S(2)}) %all-to-all-start.2) | async-done | bytes 2097184 | tf_op jit(solution)/shard_map/all_to_all | solution.py:93
  89.3 33.0 %all-to-all-done = f32[16,1,32768]{2,1,0:T(1,128)} async-done(((f32[16,1,32768]{2,1,0:T(1,128)}), f32[16,1,32768]{2,1,0:T(1,128)}, u32[]{:S(2)}, u32[]{:S(2)}) %all-to-all-start) | async-done | bytes 2097184 | tf_op jit(solution)/shard_map/all_to_all | solution.py:94
  141.5 33.2 %all-to-all-done.4 = f32[16,1,32768]{2,1,0:T(1,128)} async-done(((f32[16,1,32768]{2,1,0:T(1,128)}), f32[16,1,32768]{2,1,0:T(1,128)}, u32[]{:S(2)}, u32[]{:S(2)}) %all-to-all-start.4) | async-done | bytes 2097184 | tf_op jit(solution)/shard_map/all_to_all | solution.py:95
  182.8 7.3 %reduce.2 = f32[16,32768]{1,0:T(8,128)S(1)} reduce(f32[16,1,32768]{2,1,0:T(1,128)} %all-to-all-done.2, f32[]{:T(128)} %broadcast.567), dimensions={1}, to_apply=%all_to_all.155.reduce_sub_computation | reduce | bytes 4194308 | tf_op jit(solution)/shard_map/all_to_all | solution.py:93
  193.2 6.6 copy.141
  204.9 22.4 %all-to-all-done.6 = f32[16,1,32768]{2,1,0:T(1,128)} async-done(((f32[16,1,32768]{2,1,0:T(1,128)}), f32[16,1,32768]{2,1,0:T(1,128)}, u32[]{:S(2)}, u32[]{:S(2)}) %all-to-all-start.6) | async-done | bytes 2097184 | tf_op jit(solution)/shard_map/all_to_all | solution.py:96
  239.2 7.3 %reduce.3 = f32[16,32768]{1,0:T(8,128)S(1)} reduce(f32[16,1,32768]{2,1,0:T(1,128)} %all-to-all-done, f32[]{:T(128)} %broadcast.567), dimensions={1}, to_apply=%all_to_all.148.reduce_sub_computation | reduce | bytes 4194308 | tf_op jit(solution)/shard_map/all_to_all | solution.py:94
  249.5 6.6 copy.140
  266.4 7.3 %reduce = f32[16,32768]{1,0:T(8,128)S(1)} reduce(f32[16,1,32768]{2,1,0:T(1,128)} %all-to-all-done.4, f32[]{:T(128)} %broadcast.567), dimensions={1}, to_apply=%all_to_all.162.reduce_sub_computation | reduce | bytes 4194308 | tf_op jit(solution)/shard_map/all_to_all | solution.py:95
  288.5 7.3 %reduce.1 = f32[16,32768]{1,0:T(8,128)S(1)} reduce(f32[16,1,32768]{2,1,0:T(1,128)} %all-to-all-done.6, f32[]{:T(128)} %broadcast.567), dimensions={1}, to_apply=%all_to_all.169.reduce_sub_computation | reduce | bytes 4194308 | tf_op jit(solution)/shard_map/all_to_all | solution.py:96
  299.1 6.6 copy.143
  350.9 6.7 all-to-all-done.5
  452.4 8.8 %reshape.206 = f32[2,1,262144]{2,1,0:T(1,128)} reshape(f32[2048,2,4,32]{3,2,1,0:T(4,128)} %bitcast.251) | data formatting | bytes 4194304
  479.7 8.8 %reshape.202 = f32[2,1,262144]{2,1,0:T(1,128)} reshape(f32[2048,2,4,32]{3,2,1,0:T(4,128)} %bitcast.252) | data formatting | bytes 4194304
  494.8 8.1 %reduce.6 = f32[2,262144]{1,0:T(2,128)S(1)} reduce(f32[2,1,262144]{2,1,0:T(1,128)} %all-to-all-done.8, f32[]{:T(128)} %broadcast.567), dimensions={1}, to_apply=%all_to_all.176.reduce_sub_computation | reduce | bytes 4194308 | tf_op jit(solution)/shard_map/all_to_all | solution.py:143
  503.0 8.2 %reshape.207 = f32[2048,2,4,32]{3,2,1,0:T(4,128)} reshape(f32[2,262144]{1,0:T(2,128)S(1)} %reduce.6) | data formatting | bytes 4194304
  511.2 6.9 copy.145
  520.0 7.5 %copy.116 = f32[32,2,8,1024]{0,2,1,3:T(8,128)} copy(f32[32,2,8,1024]{3,0,2,1:T(8,128)} %bitcast.267) | data formatting | bytes 4194304 | tf_op jit(solution)/shard_map/all_to_all | solution.py:143
  527.5 8.6 %reshape.208 = f32[16,1,32768]{2,1,0:T(1,128)} reshape(f32[1024,2,8,32]{3,2,1,0:T(8,128)} %bitcast.254) | data formatting | bytes 4194304
  536.1 7.7 %all-to-all-start.9 = ((f32[16,1,32768]{2,1,0:T(1,128)}), f32[16,1,32768]{2,1,0:T(1,128)}, u32[]{:S(2)}, u32[]{:S(2)}) async-start(f32[16,1,32768]{2,1,0:T(1,128)} %reshape.208), calls=%async_computation.9 | async-start | bytes 4194304 | tf_op jit(solution)/shard_map/all_to_all | solution.py:142
  543.8 8.1 %reduce.4 = f32[2,262144]{1,0:T(2,128)S(1)} reduce(f32[2,1,262144]{2,1,0:T(1,128)} %all-to-all-done.10, f32[]{:T(128)} %broadcast.567), dimensions={1}, to_apply=%all_to_all.184.reduce_sub_computation | reduce | bytes 4194308 | tf_op jit(solution)/shard_map/all_to_all | solution.py:150
  552.0 8.2 %reshape.203 = f32[2048,2,4,32]{3,2,1,0:T(4,128)} reshape(f32[2,262144]{1,0:T(2,128)S(1)} %reduce.4) | data formatting | bytes 4194304
  560.2 6.9 copy.149
  569.0 7.5 %copy.123 = f32[32,2,8,1024]{0,2,1,3:T(8,128)} copy(f32[32,2,8,1024]{3,0,2,1:T(8,128)} %bitcast.269) | data formatting | bytes 4194304 | tf_op jit(solution)/shard_map/all_to_all | solution.py:150
  576.5 8.6 %reshape.204 = f32[16,1,32768]{2,1,0:T(1,128)} reshape(f32[1024,2,8,32]{3,2,1,0:T(8,128)} %bitcast.256) | data formatting | bytes 4194304
  599.4 7.3 %reduce.7 = f32[16,32768]{1,0:T(8,128)S(1)} reduce(f32[16,1,32768]{2,1,0:T(1,128)} %all-to-all-done.9, f32[]{:T(128)} %broadcast.567), dimensions={1}, to_apply=%all_to_all.180.reduce_sub_computation | reduce | bytes 4194308 | tf_op jit(solution)/shard_map/all_to_all | solution.py:142
  611.5 7.0 copy.156
  618.5 25.6 %all-to-all-done.11 = f32[16,1,32768]{2,1,0:T(1,128)} async-done(((f32[16,1,32768]{2,1,0:T(1,128)}), f32[16,1,32768]{2,1,0:T(1,128)}, u32[]{:S(2)}, u32[]{:S(2)}) %all-to-all-start.11) | async-done | bytes 2097184 | tf_op jit(solution)/shard_map/all_to_all | solution.py:149
  644.1 7.3 %reduce.5 = f32[16,32768]{1,0:T(8,128)S(1)} reduce(f32[16,1,32768]{2,1,0:T(1,128)} %all-to-all-done.11, f32[]{:T(128)} %broadcast.567), dimensions={1}, to_apply=%all_to_all.188.reduce_sub_computation | reduce | bytes 4194308 | tf_op jit(solution)/shard_map/all_to_all | solution.py:149
  656.2 6.9 copy.157
  663.1 15.3 %convolution_bitcast_fusion.1 = f32[2,1,8,64,512]{4,3,2,0,1:T(8,128)S(1)} fusion(f32[512,2,8,64]{3,0,2,1:T(8,128)} %bitcast.259, f32[512,512]{1,0:T(8,128)S(1)} %copy-done.20), kind=kOutput, calls=%fused_computation.57 | convolution fusion | flops 3221225472 | bytes 5242880 | tf_op jit(solution)/shard_map/zsqp,jz->sqpj/dot_general | solution.py:157
  678.5 13.3 %convolution_bitcast_fusion = f32[2,1,8,64,512]{4,3,2,0,1:T(8,128)S(1)} fusion(f32[512,2,8,64]{3,0,2,1:T(8,128)S(1)} %bitcast.260, f32[512,512]{1,0:T(8,128)S(1)} %copy-done.20), kind=kOutput, calls=%fused_computation.56 | convolution fusion | flops 3221225472 | bytes 5242880 | tf_op jit(solution)/shard_map/zsqp,jz->sqpj/dot_general | solution.py:158
  (168 shorter events, 330.4 us)
Async XLA Ops:
  15.6 54.1 %all-to-all-start.2 = ((f32[16,1,32768]{2,1,0:T(1,128)}), f32[16,1,32768]{2,1,0:T(1,128)}, u32[]{:S(2)}, u32[]{:S(2)}) async-start(f32[16,1,32768]{2,1,0:T(1,128)} %reshape.198), calls=%async_computation.2 | async-start | bytes 4194304 | tf_op jit(solution)/shard_map/all_to_all | solution.py:93
  36.5 38.4 %copy-start.19 = (f32[512,512]{1,0:T(8,128)S(1)}, f32[512,512]{1,0:T(8,128)}, u32[]{:S(2)}) copy-start(f32[512,512]{1,0:T(8,128)} %param.12) | copy-start | bytes 3145732
  69.7 52.6 %all-to-all-start = ((f32[16,1,32768]{2,1,0:T(1,128)}), f32[16,1,32768]{2,1,0:T(1,128)}, u32[]{:S(2)}, u32[]{:S(2)}) async-start(f32[16,1,32768]{2,1,0:T(1,128)} %reshape.200), calls=%async_computation | async-start | bytes 4194304 | tf_op jit(solution)/shard_map/all_to_all | solution.py:94
  122.3 52.4 %all-to-all-start.4 = ((f32[16,1,32768]{2,1,0:T(1,128)}), f32[16,1,32768]{2,1,0:T(1,128)}, u32[]{:S(2)}, u32[]{:S(2)}) async-start(f32[16,1,32768]{2,1,0:T(1,128)} %reshape.194), calls=%async_computation.4 | async-start | bytes 4194304 | tf_op jit(solution)/shard_map/all_to_all | solution.py:95
  141.5 38.5 %copy-start.24 = (f32[3,32,2048]{2,1,0:T(8,128)S(1)}, f32[3,32,2048]{2,1,0:T(8,128)}, u32[]{:S(2)}) copy-start(f32[3,32,2048]{2,1,0:T(8,128)} %param.15) | copy-start | bytes 2359300
  174.7 52.6 %all-to-all-start.6 = ((f32[16,1,32768]{2,1,0:T(1,128)}), f32[16,1,32768]{2,1,0:T(1,128)}, u32[]{:S(2)}, u32[]{:S(2)}) async-start(f32[16,1,32768]{2,1,0:T(1,128)} %reshape.196), calls=%async_computation.6 | async-start | bytes 4194304 | tf_op jit(solution)/shard_map/all_to_all | solution.py:96
  227.3 34.0 %all-to-all-start.3 = ((f32[32,2,8,1024]{3,1,0,2:T(2,128)}), f32[32,2,8,1024]{3,1,0,2:T(2,128)}, u32[]{:S(2)}, u32[]{:S(2)}) async-start(f32[32,2,8,1024]{3,1,0,2:T(2,128)} %reshape.191), calls=%async_computation.3 | async-start | bytes 4194304 | tf_op jit(solution)/shard_map/all_to_all | solution.py:99
  234.9 2.9 copy-start.26
  234.9 2.9 copy-start.28
  236.1 2.9 copy-start.23
  261.3 67.8 %all-to-all-start.1 = ((f32[32,2,8,1024]{3,1,0,2:T(2,128)}), f32[32,2,8,1024]{3,1,0,2:T(2,128)}, u32[]{:S(2)}, u32[]{:S(2)}) async-start(f32[32,2,8,1024]{3,1,0,2:T(2,128)} %reshape.190), calls=%async_computation.1 | async-start | bytes 4194304 | tf_op jit(solution)/shard_map/all_to_all | solution.py:100
  329.1 28.5 %all-to-all-start.5 = ((f32[32,2,8,1024]{3,1,0,2:T(2,128)}), f32[32,2,8,1024]{3,1,0,2:T(2,128)}, u32[]{:S(2)}, u32[]{:S(2)}) async-start(f32[32,2,8,1024]{3,1,0,2:T(2,128)} %reshape.192), calls=%async_computation.5 | async-start | bytes 4194304 | tf_op jit(solution)/shard_map/all_to_all | solution.py:101
  343.3 2.2 copy-start.12
  357.7 30.3 %all-to-all-start.7 = ((f32[32,2,8,1024]{3,1,0,2:T(2,128)}), f32[32,2,8,1024]{3,1,0,2:T(2,128)}, u32[]{:S(2)}, u32[]{:S(2)}) async-start(f32[32,2,8,1024]{3,1,0,2:T(2,128)} %reshape.193), calls=%async_computation.7 | async-start | bytes 4194304 | tf_op jit(solution)/shard_map/all_to_all | solution.py:102
  372.9 5.0 copy-start.10
  377.9 3.2 copy-start.3
  397.6 4.4 copy-start.9
  397.6 4.4 copy-start.13
  423.4 2.4 copy-start.21
  423.4 2.4 copy-start.22
  461.2 27.3 %all-to-all-start.8 = ((f32[2,1,262144]{2,1,0:T(1,128)}), f32[2,1,262144]{2,1,0:T(1,128)}, u32[]{:S(2)}, u32[]{:S(2)}) async-start(f32[2,1,262144]{2,1,0:T(1,128)} %reshape.206), calls=%async_computation.8 | async-start | bytes 4194304 | tf_op jit(solution)/shard_map/all_to_all | solution.py:143
  466.2 3.7 copy-start.6
  488.5 47.6 %all-to-all-start.10 = ((f32[2,1,262144]{2,1,0:T(1,128)}), f32[2,1,262144]{2,1,0:T(1,128)}, u32[]{:S(2)}, u32[]{:S(2)}) async-start(f32[2,1,262144]{2,1,0:T(1,128)} %reshape.202), calls=%async_computation.10 | async-start | bytes 4194304 | tf_op jit(solution)/shard_map/all_to_all | solution.py:150
  536.1 55.1 %all-to-all-start.9 = ((f32[16,1,32768]{2,1,0:T(1,128)}), f32[16,1,32768]{2,1,0:T(1,128)}, u32[]{:S(2)}, u32[]{:S(2)}) async-start(f32[16,1,32768]{2,1,0:T(1,128)} %reshape.208), calls=%async_computation.9 | async-start | bytes 4194304 | tf_op jit(solution)/shard_map/all_to_all | solution.py:142
  585.1 12.3 %copy-start.25 = (f32[512]{0:T(512)S(1)}, f32[512]{0:T(512)}, u32[]{:S(2)}) copy-start(f32[512]{0:T(512)} %param.14) | copy-start | bytes 6148
  585.1 12.6 %copy-start.27 = (f32[2]{0:T(128)S(1)}, f32[2]{0:T(128)}, u32[]{:S(2)}) copy-start(f32[2]{0:T(128)} %param.18) | copy-start | bytes 28
  591.2 52.9 %all-to-all-start.11 = ((f32[16,1,32768]{2,1,0:T(1,128)}), f32[16,1,32768]{2,1,0:T(1,128)}, u32[]{:S(2)}, u32[]{:S(2)}) async-start(f32[16,1,32768]{2,1,0:T(1,128)} %reshape.204), calls=%async_computation.11 | async-start | bytes 4194304 | tf_op jit(solution)/shard_map/all_to_all | solution.py:149
  656.2 6.9 copy-start.20
  663.1 15.4 %copy-start.11 = (f32[16,32,2,8,64]{4,1,0,3,2:T(8,128)S(1)}, f32[16,32,2,8,64]{4,1,0,3,2:T(8,128)}, u32[]{:S(2)}) copy-start(f32[16,32,2,8,64]{4,1,0,3,2:T(8,128)} %copy.157) | copy-start | bytes 6291460
  678.5 13.4 %copy-start.2 = (f32[2,2,8,64,512]{4,3,2,1,0:T(8,128)S(1)}, f32[2,2,8,64,512]{4,3,2,1,0:T(8,128)}, u32[]{:S(2)}) copy-start(f32[2,2,8,64,512]{4,3,2,1,0:T(8,128)} %param.10) | copy-start | bytes 12582916
  678.5 13.4 %copy-start.16 = (f32[2,8,64,512]{3,2,1,0:T(8,128)S(1)}, f32[2,8,64,512]{3,2,1,0:T(8,128)}, u32[]{:S(2)}) copy-start(f32[2,8,64,512]{3,2,1,0:T(8,128)} %multiply_add_fusion) | copy-start | bytes 6291460
  693.5 2.6 copy-start.1
  (9 other events, 18.1 us)
where the time goes:
time: 707 us; the launch traced here: 696 us
  local copies, waits for them, and re-layouts  266 us (38%)
  waiting for transfers between devices  160 us (23%)
  matrix products  136 us (19%)
  starting transfers between devices  67.7 us (10%)
  other arithmetic  65.1 us (9%)
    unnamed x75, local copies, waits for them, and re-layouts  99.1 us
    all_to_all x1, waiting for transfers between devices, on_device(): lax.all_to_all(slope_real, 'col', split_axis=0, concat_axis=3, tiled=True)  33.2 us
    all_to_all x1, waiting for transfers between devices, on_device(): lax.all_to_all(value_real, 'col', split_axis=0, concat_axis=3, tiled=True)  33.1 us
    all_to_all x1, waiting for transfers between devices, on_device(): lax.all_to_all(value_imag, 'col', split_axis=0, concat_axis=3, tiled=True)  33 us
    all_to_all x1, waiting for transfers between devices, on_device(): lax.all_to_all(lax.all_to_all(spectra_imag, 'row', split_axis=3, concat_a...  25.6 us
    dot_general x8, matrix products, contract(): jnp.einsum(form, left_imag, right_imag, precision=highest)  24.6 us
    all_to_all x1, waiting for transfers between devices, on_device(): lax.all_to_all(slope_imag, 'col', split_axis=0, concat_axis=3, tiled=True)  22.4 us
    dot_general x8, matrix products, contract(): jnp.einsum(form, left_real, right_real, precision=highest)  21.7 us
  transfers between devices with their start and end apart: 12, of which 7 were waited for; matrix products, arithmetic and copies ran while one was open for 47% of the time, Pallas kernels for 0%

commit v1 on v0

--- a/solution.py
+++ b/solution.py
@@ -1,8 +1,13 @@
+import functools
 import math
 
 import jax
 import jax.numpy as jnp
+import ml_dtypes
+import numpy as np
 from jax import lax
+from jax.experimental import pallas as pl
+from jax.experimental.pallas import tpu as pltpu
 from jax.sharding import PartitionSpec as P
 
 highest = lax.Precision.HIGHEST
@@ -165,6 +170,278 @@
     return (coefficients - time_step * forcing) / denominator
 
 
+def wide_tables(total):
+    short = total // lane_width
+    points = np.arange(lane_width)[None, :, None]
+    waves = np.arange(lane_width)[None, None, :] * short + np.arange(short)[:, None, None]
+    angles = (points * waves % total) * (2.0 * math.pi / total)
+    scale = 1.0 / math.sqrt(total)
+    cosines, sines = np.cos(angles) * scale, np.sin(angles) * scale
+    inverse = np.concatenate(
+        [
+            np.concatenate([cosines, -sines], 2),
+            np.concatenate([sines, cosines], 2),
+        ],
+        1,
+    )
+    tables = []
+    for table in (inverse, np.swapaxes(inverse, 1, 2)):
+        high = table.astype(ml_dtypes.bfloat16)
+        low = (table - high.astype(np.float64)).astype(ml_dtypes.bfloat16)
+        tables += [high, low]
+    return tables
+
+
+def short_transform(values, direction):
+    count = len(values)
+    if count == 1:
+        return values
+    even = short_transform(values[0::2], direction)
+    odd = short_transform(values[1::2], direction)
+    first, second = [], []
+    for index in range(count // 2):
+        real, imag = odd[index]
+        if index == 0:
+            pass
+        elif 4 * index == count:
+            real, imag = (-imag, real) if direction > 0 else (imag, -real)
+        else:
+            angle = direction * 2.0 * math.pi * index / count
+            turn_real, turn_imag = math.cos(angle), math.sin(angle)
+            real, imag = (
+                real * turn_real - imag * turn_imag,
+                real * turn_imag + imag * turn_real,
+            )
+        base_real, base_imag = even[index]
+        first.append((base_real + real, base_imag + imag))
+        second.append((base_real - real, base_imag - imag))
+    return first + second
+
+
+def split_dot(table_high, table_low, value):
+    high = value.astype(jnp.bfloat16)
+    low = (value - high.astype(jnp.float32)).astype(jnp.bfloat16)
+    dot = functools.partial(jnp.dot, preferred_element_type=jnp.float32)
+    return dot(table_high, high) + (dot(table_high, low) + dot(table_low, high))
+
+
+def section_kernel(
+    total,
+    which_ref,
+    span_ref,
+    value_own,
+    value_other,
+    slope_own,
+    slope_other,
+    flow_ref,
+    inverse_high,
+    inverse_low,
+    forward_high,
+    forward_low,
+    kept_ref,
+    sent_ref,
+    fields,
+    spectra,
+):
+    short = total // lane_width
+    lanes = lane_width
+    first = which_ref[0] == 0
+    span_wave = span_ref[0]
+
+    def waves_at(residue):
+        index = lax.broadcasted_iota(jnp.int32, (lanes, lanes), 0) * short + residue
+        return jnp.where(index < total // 2, index, index - total)
+
+    @pl.loop(0, short)
+    def _(residue):
+        rows = pl.ds(residue, lanes, stride=short)
+        own, other = value_own[rows, :], value_other[rows, :]
+        value_real, value_imag = jnp.where(first, own, other), jnp.where(first, other, own)
+        own, other = slope_own[rows, :], slope_other[rows, :]
+        slope_real, slope_imag = jnp.where(first, own, other), jnp.where(first, other, own)
+        zonal = waves_at(residue).astype(jnp.float32) * (2.0 * math.pi / total)
+        stacked = jnp.concatenate(
+            [
+                jnp.concatenate([value_real, -zonal * value_imag, slope_real], 1),
+                jnp.concatenate([value_imag, zonal * value_real, slope_imag], 1),
+            ],
+            0,
+        )
+        fields[residue] = split_dot(inverse_high[residue], inverse_low[residue], stacked)
+
+    background = flow_ref[0, pl.ds(total + which_ref[1], 1), :]
+
+    @pl.loop(0, lanes // 8)
+    def _(chunk):
+        start = pl.multiple_of(chunk * 8, 8)
+
+        def grid_field(at):
+            columns = slice(at * lanes, (at + 1) * lanes)
+            return short_transform(
+                [
+                    (
+                        fields[e, pl.ds(start, 8), columns],
+                        fields[e, pl.ds(start + lanes, 8), columns],
+                    )
+                    for e in range(short)
+                ],
+                1.0,
+            )
+
+        def flow(axis, d):
+            return flow_ref[axis, pl.ds(start + d * lanes, 8), :]
+
+        advect = []
+        for d, (real, imag) in enumerate(grid_field(1)):
+            zonal_flow = flow(0, d)
+            advect.append((zonal_flow * real, zonal_flow * imag))
+        for d, (real, imag) in enumerate(grid_field(0)):
+            span_flow = flow(1, d) * span_wave
+            advect[d] = (advect[d][0] - span_flow * imag, advect[d][1] + span_flow * real)
+        for d, (real, imag) in enumerate(grid_field(2)):
+            rise_flow = flow(2, d)
+            advect[d] = (
+                advect[d][0] + rise_flow * (real + background),
+                advect[d][1] + rise_flow * imag,
+            )
+        for e, (real, imag) in enumerate(short_transform(advect, -1.0)):
+            spectra[e, pl.ds(start, 8), :] = real
+            spectra[e, pl.ds(start + lanes, 8), :] = imag
+
+    @pl.loop(0, short)
+    def _(residue):
+        rows = pl.ds(residue, lanes, stride=short)
+        result = split_dot(forward_high[residue], forward_low[residue], spectra[residue])
+        retained = jnp.abs(waves_at(residue)) <= total // 3
+        real = jnp.where(retained, result[:lanes], 0.0)
+        imag = jnp.where(retained, result[lanes:], 0.0)
+        kept_ref[rows, :] = jnp.where(first, real, imag)
+        sent_ref[rows, :] = jnp.where(first, imag, real)
+
+
+def advance_waves(total, levels, which, span_wave, own, other, flow):
+    lanes = lane_width
+    blocks = levels // lanes
+    short = total // lanes
+    tables = [jnp.asarray(table) for table in wide_tables(total)]
+    value_spec = pl.BlockSpec((total, lanes), lambda i: (0, i))
+    slope_spec = pl.BlockSpec((total, lanes), lambda i: (0, blocks + i))
+    table_spec = pl.BlockSpec((short, 2 * lanes, 2 * lanes), lambda i: (0, 0, 0))
+    scalars = pl.BlockSpec(memory_space=pltpu.SMEM)
+    return pl.pallas_call(
+        functools.partial(section_kernel, total),
+        grid=(blocks,),
+        in_specs=[
+            scalars,
+            scalars,
+            value_spec,
+            value_spec,
+            slope_spec,
+            slope_spec,
+            pl.BlockSpec((3, flow.shape[1], lanes), lambda i: (0, 0, i)),
+        ]
+        + [table_spec] * 4,
+        out_specs=[value_spec, value_spec],
+        out_shape=[jax.ShapeDtypeStruct((total, levels), jnp.float32)] * 2,
+        scratch_shapes=[
+            pltpu.VMEM((short, 2 * lanes, 3 * lanes), jnp.float32),
+            pltpu.VMEM((short, 2 * lanes, lanes), jnp.float32),
+        ],
+        compiler_params=pltpu.CompilerParams(vmem_limit_bytes=56 * 1024 * 1024),
+    )(which, span_wave, own, other, own, other, flow, *tables)
+
+
+def by_section(
+    coefficients,
+    vertical_modes,
+    mode_slopes,
+    dual_modes,
+    eigenvalues,
+    velocity,
+    gradient,
+    span_wavenumbers,
+    implicit_rates,
+    time_step,
+):
+    high = lax.Precision.HIGH
+    axes = ("row", "col")
+    col_count = lax.axis_size("col")
+    device_count = lax.axis_size("row") * col_count
+    scalars, parts, spans, local_waves, modes = coefficients.shape
+    total = local_waves * device_count
+    level_count = dual_modes.shape[1]
+    half = level_count // 2
+    col = lax.axis_index("col")
+    device = lax.axis_index("row") * col_count + col
+    part, section = device % 2, device // 2
+    scalar, span = section // spans, section % spans
+    partners = [(at, at ^ 1) for at in range(col_count)]
+
+    pairs = col_count // 2
+    level_rows = velocity.shape[1]
+    marks = jnp.pad(
+        jnp.transpose(gradient)[None], ((0, 2), (0, 0), (0, lane_width - scalars))
+    )
+    flow = jnp.concatenate([velocity, marks], 2)
+    flow = lax.ppermute(
+        flow, "col", [(at, 2 * (at % pairs) + at // pairs) for at in range(col_count)]
+    )
+    groups = [list(range(0, col_count, 2)), list(range(1, col_count, 2))]
+    flow = lax.all_gather(flow, "col", axis_index_groups=groups)
+    flow = jnp.transpose(flow, (1, 3, 0, 2)).reshape(3, total + lane_width, pairs * level_rows)
+
+    sent = jnp.swapaxes(coefficients, 1, 2).reshape(device_count, local_waves, modes)
+    lines = lax.all_to_all(sent, axes, 0, 0, tiled=True).reshape(total, modes)
+
+    def half_of(table, which, axis):
+        return lax.dynamic_slice_in_dim(table, which * half, half, axis)
+
+    def to_levels(which):
+        table = jnp.concatenate(
+            [half_of(vertical_modes, which, 0), half_of(mode_slopes, which, 0)], 0
+        )
+        return jnp.einsum("pj,zj->pz", lines, table, precision=high)
+
+    other = lax.ppermute(to_levels(1 - part), "col", partners)
+    own = to_levels(part)
+    which = jnp.stack([part, scalar]).astype(jnp.int32)
+    kept, passed = advance_waves(
+        total, half, which, span_wavenumbers[span][None], own, other, flow
+    )
+    received = lax.ppermute(passed, "col", partners)
+    forcing = jnp.einsum(
+        "pz,jz->pj", kept, half_of(dual_modes, part, 1), precision=high
+    ) + jnp.einsum("pz,jz->pj", received, half_of(dual_modes, 1 - part, 1), precision=high)
+    forcing = lax.all_to_all(
+        forcing.reshape(device_count, local_waves, modes), axes, 0, 0, tiled=True
+    )
+    forcing = jnp.swapaxes(
+        forcing.reshape(scalars, spans, parts, local_waves, modes), 1, 2
+    )
+    zonal_waves = signed_waves(total).astype(jnp.float32) * (2.0 * math.pi / total)
+    own_waves = lax.dynamic_slice_in_dim(zonal_waves, device * local_waves, local_waves)
+    denominator = 1.0 + implicit_rates[:, None, None, None, None] * (
+        eigenvalues[None, None, None, None, :]
+        + own_waves[None, None, None, :, None] ** 2
+        + span_wavenumbers[None, None, :, None, None] ** 2
+    )
+    return (coefficients - time_step * forcing) / denominator
+
+
+def program(*arrays):
+    coefficients, levels = arrays[0], arrays[3].shape[1]
+    col_count = lax.axis_size("col")
+    device_count = lax.axis_size("row") * col_count
+    scalars, _, spans, _, _ = coefficients.shape
+    fits = (
+        device_count == 2 * scalars * spans
+        and col_count % 2 == 0
+        and (levels // 2) % lane_width == 0
+        and coefficients.shape[3] * device_count == 16 * lane_width
+    )
+    return by_section(*arrays) if fits else on_device(*arrays)
+
+
 def solution(mesh):
     in_specs = (
         P(None, None, None, ("row", "col"), None),
@@ -180,5 +457,5 @@
     )
     out_specs = P(None, None, None, ("row", "col"), None)
     return jax.shard_map(
-        on_device, mesh=mesh, in_specs=in_specs, out_specs=out_specs, check_vma=False
-    )
+        program, mesh=mesh, in_specs=in_specs, out_specs=out_specs, check_vma=False
+    )

time: 707 us -> 411 us (0.58)
  local copies, waits for them, and re-layouts: 266 us -> 25 us
  waiting for transfers between devices: 160 us -> 282 us
  matrix products: 136 us -> 20.8 us
  other arithmetic: 65.1 us -> 5.91 us
  starting transfers between devices: 67.7 us -> 18.6 us
  Pallas kernels: 0 us -> 38.9 us
  between operations: 1.68 us -> 14.2 us
    dot_general x38 -> x4, matrix products: 136 us -> 20.8 us  [the longest x2 14.9 us: to_levels(): return jnp.einsum('pj,zj->pz', lines, table, precision=high)]
    all_to_all x25 -> x0, local copies, waits for them, and re-layouts: 115 us -> none  [the longest x3 16.3 us: on_device(): lax.all_to_all(spectra_real, 'row', split_axis=3, concat_axis=2, tiled=True)]
    ppermute x0 -> x3, waiting for transfers between devices: none -> 109 us  [the longest x1 105 us: by_section(): lax.ppermute(flow, 'col', [(at, 2 * (at % pairs) + at // pairs) for at in...]
    unnamed x75 -> x20, local copies, waits for them, and re-layouts: 99.1 us -> 6.44 us
    all_gather x0 -> x1, waiting for transfers between devices: none -> 83.5 us  [by_section(): flow = lax.all_gather(flow, 'col', axis_index_groups=groups)]
    all_to_all x12 -> x2, waiting for transfers between devices: 160 us -> 89.3 us  [the longest x1 89.3 us: by_section(): lax.all_to_all(forcing.reshape(device_count, local_waves, modes), axes, 0...]
    all_to_all x8 -> x0, other arithmetic: 60.2 us -> none  [the longest x1 8.14 us: on_device(): lax.all_to_all(spectra_real, 'row', split_axis=3, concat_axis=2, tiled=True)]
    all_to_all x12 -> x2, starting transfers between devices: 67.7 us -> 12.8 us  [the longest x1 6.48 us: by_section(): lax.all_to_all(forcing.reshape(device_count, local_waves, modes), axes, 0...]
  transfers between devices with their start and end apart: 12 -> 6, of which waited for: 7 -> 4; matrix products, arithmetic and copies ran while one was open for 47% -> 8% of each run, Pallas kernels for 0% -> 0%
where the time goes in v1:
time: 411 us; the launch traced here: 405 us
  waiting for transfers between devices  282 us (69%)
  Pallas kernels  38.9 us (9%)
  local copies, waits for them, and re-layouts  25 us (6%)
  matrix products  20.8 us (5%)
  starting transfers between devices  18.6 us (5%)
  between operations  14.2 us (3%)
  other arithmetic  5.91 us (1%)
    ppermute x1, waiting for transfers between devices, by_section(): lax.ppermute(flow, 'col', [(at, 2 * (at % pairs) + at // pairs) for at in...  105 us
    all_to_all x1, waiting for transfers between devices, by_section(): lax.all_to_all(forcing.reshape(device_count, local_waves, modes), axes, 0...  89.3 us
    all_gather x1, waiting for transfers between devices, by_section(): flow = lax.all_gather(flow, 'col', axis_index_groups=groups)  83.5 us
    pallas_call x1, Pallas kernels, advance_waves(): pl.pallas_call(functools.partial(section_kernel, total), grid=(blocks,),...  38.9 us
    dot_general x2, matrix products, to_levels(): return jnp.einsum('pj,zj->pz', lines, table, precision=high)  14.9 us
  transfers between devices with their start and end apart: 6, of which 4 were waited for; matrix products, arithmetic and copies ran while one was open for 8% of the time, Pallas kernels for 0%

profile of v1, /device:TPU:15, one launch (start us, length us, event | category | flops | bytes accessed | tf_op | source)
XLA Modules:
  0.0 405.3 jit_solution(4862587694981000534)
XLA Ops:
  6.5 5.0 %copy.40 = f32[2,2,8,64,512]{4,3,1,2,0:T(8,128)} copy(f32[2,2,8,64,512]{4,3,2,1,0:T(8,128)} %param.14) | data formatting | bytes 8388608 | tf_op args[0]
  11.5 6.3 %all-to-all-start = ((f32[32,64,512]{2,1,0:T(8,128)}), f32[32,64,512]{2,1,0:T(8,128)}, u32[]{:S(2)}, u32[]{:S(2)}) async-start(f32[32,64,512]{2,1,0:T(8,128)} %bitcast.27), calls=%async_computation | async-start | bytes 8388608 | tf_op jit(solution)/shard_map/all_to_all | solution.py:394
  17.9 0.0 all-gather.3.cloned.1.call-start
  17.9 0.1 copy.44
  18.0 0.1 select_maximum_fusion
  18.1 4.3 %collective-permute-start.1 = (f32[3,32,2176]{2,1,0:T(8,128)S(1)}, f32[3,32,2176]{2,1,0:T(8,128)S(1)}, u32[]{:S(2)}, u32[]{:S(2)}) collective-permute-start(f32[3,32,2176]{2,1,0:T(8,128)S(1)} %select_maximum_fusion), channel_id=1, source_target_pairs={{0,0},{1,2},{2,4},{3,6},{4,8},{5,10},{6,12},{7,14},{8,1},{9,3},{10... | collective-permute-start | bytes 2506760 | tf_op jit(solution)/shard_map/ppermute | solution.py:386
  22.4 105.0 %collective-permute-done.1 = f32[3,32,2176]{2,1,0:T(8,128)S(1)} collective-permute-done((f32[3,32,2176]{2,1,0:T(8,128)S(1)}, f32[3,32,2176]{2,1,0:T(8,128)S(1)}, u32[]{:S(2)}, u32[]{:S(2)}) %collective-permute-start.1) | collective-permute-done | bytes 835616 | tf_op jit(solution)/shard_map/ppermute | solution.py:386
  127.5 0.9 copy-done.3
  128.4 0.0 all-gather.3.cloned.1.call-update
  128.4 1.7 constant_dynamic-slice_fusion
  130.1 0.0 copy-start.8
  130.1 7.4 %convolution_bitcast_fusion = f32[2048,512]{1,0:T(8,128)} fusion(f32[2048,512]{1,0:T(8,128)} %bitcast.4, f32[256,512]{1,0:T(8,128)S(1)} %get-tuple-element.11, f32[256,512]{1,0:T(8,128)S(1)} %get-tuple-element.14), kind=kOutput, calls=%fused_computation.2 | convolution fusion | flops 3221487616 | bytes 9437184 | tf_op jit(solution)/shard_map/pj,zj->pz/dot_general | solution.py:403
  137.5 0.6 dynamic_slice.24.span_ref
  138.1 0.6 pad_add_fusion.which_ref
  138.7 7.5 %convolution_bitcast_fusion.1.value_own.slope_own = f32[2048,512]{1,0:T(8,128)} fusion(f32[2048,512]{1,0:T(8,128)} %bitcast.4, f32[256,512]{1,0:T(8,128)S(1)} %get-tuple-element.12, f32[256,512]{1,0:T(8,128)S(1)} %get-tuple-element.13), kind=kOutput, calls=%fused_computation.3 | convolution fusion | flops 3221487616 | bytes 9437184 | tf_op jit(solution)/shard_map/pj,zj->pz/dot_general | solution.py:403
  146.2 83.5 %all-gather.3.cloned.1.call-done = f32[24,32,2176]{2,1,0:T(8,128)} async-done(((f32[3,32,2176]{2,1,0:T(8,128)}), f32[24,32,2176]{2,1,0:T(8,128)}) %all-gather.3.cloned.1.call-update) | async-done | bytes 6684688 | tf_op jit(solution)/shard_map/all_gather | solution.py:390
  229.7 6.2 %copy.38 = f32[3,2176,8,32]{1,3,2,0:T(8,128)} copy(f32[3,2176,8,32]{1,3,0,2:T(8,128)} %bitcast.29) | data formatting | bytes 13369344 | tf_op jit(solution)/shard_map/transpose | solution.py:391
  235.9 7.5 %copy.39.flow_ref = f32[3,2176,256]{2,1,0:T(8,128)} copy(f32[3,2176,256]{1,2,0:T(8,128)} %bitcast.25) | data formatting | bytes 13369344 | tf_op jit(solution)/shard_map/reshape | solution.py:391
  243.4 38.9 %shard_map.136 = (f32[2048,256]{1,0:T(8,128)}, f32[2048,256]{1,0:T(8,128)}) custom-call(s32[2]{0:T(128)} %pad_add_fusion.which_ref, f32[1]{0:T(128)} %dynamic_slice.24.span_ref, f32[2048,512]{1,0:T(8,128)} %convolution_bitcast_fusion.1.value_own.slope_own, f32[2048,512]{1,0:T(8,128)} %collective-permute-done.value_other.slope_other, ...), custom_call_target="tpu_custom_call" | custom-call | tf_op jit(solution)/shard_map/pallas_call | solution.py:331
  282.3 1.4 collective-permute-start.2
  283.7 4.0 collective-permute-done.2
  287.7 1.9 fusion.6
  289.7 4.0 convolution_add_fusion
  293.7 6.5 %all-to-all-start.1 = ((f32[32,64,512]{2,1,0:T(8,128)}), f32[32,64,512]{2,1,0:T(8,128)}, u32[]{:S(2)}, u32[]{:S(2)}) async-start(f32[32,64,512]{2,1,0:T(8,128)} %bitcast.28), calls=%async_computation.1 | async-start | bytes 8388608 | tf_op jit(solution)/shard_map/all_to_all | solution.py:415
  300.9 0.1 broadcast_add_fusion.1
  301.0 0.2 broadcast_add_fusion
  301.2 0.3 multiply_add_fusion
  301.5 89.3 %all-to-all-done.1 = f32[32,64,512]{2,1,0:T(8,128)} async-done(((f32[32,64,512]{2,1,0:T(8,128)}), f32[32,64,512]{2,1,0:T(8,128)}, u32[]{:S(2)}, u32[]{:S(2)}) %all-to-all-start.1) | async-done | bytes 4194336 | tf_op jit(solution)/shard_map/all_to_all | solution.py:415
  390.8 3.0 broadcast_multiply_fusion
  393.8 0.4 copy-done.1
  394.2 1.6 subtract_divide_fusion
  395.9 2.6 copy.41
  (20 shorter events, 0.0 us)
Async XLA Ops:
  6.5 281.2 %copy-start = (f32[512,512]{1,0:T(8,128)S(1)}, f32[512,512]{1,0:T(8,128)}, u32[]{:S(2)}) copy-start(f32[512,512]{1,0:T(8,128)} %param.17) | copy-start | bytes 3145732
  11.5 6.4 %copy-start.6 = (f32[2,32]{1,0:T(2,128)S(1)}, f32[2,32]{1,0:T(2,128)}, u32[]{:S(2)}) copy-start(f32[2,32]{1,0:T(2,128)} %param.20) | copy-start | bytes 772
  11.5 6.5 %copy-start.4 = (f32[3,32,2048]{2,1,0:T(8,128)S(1)}, f32[3,32,2048]{2,1,0:T(8,128)}, u32[]{:S(2)}) copy-start(f32[3,32,2048]{2,1,0:T(8,128)} %param.19) | copy-start | bytes 2359300
  11.5 118.6 %all-to-all-start = ((f32[32,64,512]{2,1,0:T(8,128)}), f32[32,64,512]{2,1,0:T(8,128)}, u32[]{:S(2)}, u32[]{:S(2)}) async-start(f32[32,64,512]{2,1,0:T(8,128)} %bitcast.27), calls=%async_computation | async-start | bytes 8388608 | tf_op jit(solution)/shard_map/all_to_all | solution.py:394
  17.9 211.8 %all-gather.3.cloned.1.call-start = ((), (), s32[]{:S(2)}) async-start(), calls=%async_computation.2 | async-start | bytes 7520256 | tf_op jit(solution)/shard_map/all_gather | solution.py:390
  18.1 109.4 %collective-permute-start.1 = (f32[3,32,2176]{2,1,0:T(8,128)S(1)}, f32[3,32,2176]{2,1,0:T(8,128)S(1)}, u32[]{:S(2)}, u32[]{:S(2)}) collective-permute-start(f32[3,32,2176]{2,1,0:T(8,128)S(1)} %select_maximum_fusion), channel_id=1, source_target_pairs={{0,0},{1,2},{2,4},{3,6},{4,8},{5,10},{6,12},{7,14},{8,1},{9,3},{10... | collective-permute-start | bytes 2506760 | tf_op jit(solution)/shard_map/ppermute | solution.py:386
  127.5 0.9 copy-start.3
  130.1 7.4 %copy-start.8 = (f32[8]{0:T(128)S(1)}, f32[8]{0:T(128)}, u32[]{:S(2)}) copy-start(f32[8]{0:T(128)} %param.21) | copy-start | bytes 100
  137.5 105.9 %collective-permute-start = (f32[2048,512]{1,0:T(8,128)}, f32[2048,512]{1,0:T(8,128)}, u32[]{:S(2)}, u32[]{:S(2)}) collective-permute-start(f32[2048,512]{1,0:T(8,128)} %convolution_bitcast_fusion), channel_id=1, source_target_pairs={{0,1},{1,0},{2,3},{3,2},{4,5},{5,4},{6,7},{7,6},{8,9},{9,8},{10,11... | collective-permute-start | bytes 12582920 | tf_op jit(solution)/shard_map/ppermute | solution.py:405
  282.3 7.4 %copy-start.2 = (f32[2048,256]{1,0:T(8,128)S(1)}, f32[2048,256]{1,0:T(8,128)}, u32[]{:S(2)}) copy-start(f32[2048,256]{1,0:T(8,128)} %get-tuple-element.7) | copy-start | bytes 6291460
  282.3 5.4 %collective-permute-start.2 = (f32[2048,256]{1,0:T(8,128)}, f32[2048,256]{1,0:T(8,128)S(1)}, u32[]{:S(2)}, u32[]{:S(2)}) collective-permute-start(f32[2048,256]{1,0:T(8,128)} %get-tuple-element.8), channel_id=1, source_target_pairs={{0,1},{1,0},{2,3},{3,2},{4,5},{5,4},{6,7},{7,6},{8,9},{9,8},{10,11... | collective-permute-start | bytes 6291464 | tf_op jit(solution)/shard_map/ppermute | solution.py:411
  293.7 7.2 %copy-start.5 = (f32[512]{0:T(512)S(1)}, f32[512]{0:T(512)}, u32[]{:S(2)}) copy-start(f32[512]{0:T(512)} %param.18) | copy-start | bytes 6148
  293.7 7.5 %copy-start.7 = (f32[2]{0:T(128)S(1)}, f32[2]{0:T(128)}, u32[]{:S(2)}) copy-start(f32[2]{0:T(128)} %param.22) | copy-start | bytes 28
  293.7 97.1 %all-to-all-start.1 = ((f32[32,64,512]{2,1,0:T(8,128)}), f32[32,64,512]{2,1,0:T(8,128)}, u32[]{:S(2)}, u32[]{:S(2)}) async-start(f32[32,64,512]{2,1,0:T(8,128)} %bitcast.28), calls=%async_computation.1 | async-start | bytes 8388608 | tf_op jit(solution)/shard_map/all_to_all | solution.py:415
  390.8 3.4 copy-start.1
Sparse Core Ops, SparseCore 0:
  128.5 101.1 all-gather.2

commit v2 on v1

--- a/solution.py
+++ b/solution.py
@@ -383,9 +383,6 @@
         jnp.transpose(gradient)[None], ((0, 2), (0, 0), (0, lane_width - scalars))
     )
     flow = jnp.concatenate([velocity, marks], 2)
-    flow = lax.ppermute(
-        flow, "col", [(at, 2 * (at % pairs) + at // pairs) for at in range(col_count)]
-    )
     groups = [list(range(0, col_count, 2)), list(range(1, col_count, 2))]
     flow = lax.all_gather(flow, "col", axis_index_groups=groups)
     flow = jnp.transpose(flow, (1, 3, 0, 2)).reshape(3, total + lane_width, pairs * level_rows)
@@ -394,7 +391,9 @@
     lines = lax.all_to_all(sent, axes, 0, 0, tiled=True).reshape(total, modes)
 
     def half_of(table, which, axis):
-        return lax.dynamic_slice_in_dim(table, which * half, half, axis)
+        shape = table.shape[:axis] + (pairs, 2, level_rows) + table.shape[axis + 1 :]
+        taken = lax.dynamic_index_in_dim(table.reshape(shape), which, axis + 1, keepdims=False)
+        return taken.reshape(table.shape[:axis] + (half,) + table.shape[axis + 1 :])
 
     def to_levels(which):
         table = jnp.concatenate(

time: 411 us -> 384 us (0.934)
  waiting for transfers between devices: 282 us -> 260 us
  starting transfers between devices: 18.6 us -> 12.5 us
    all_to_all x1, waiting for transfers between devices: 0.01 us -> 168 us  [by_section(): lines = lax.all_to_all(sent, axes, 0, 0, tiled=True).reshape(total, modes)]
    ppermute x1 -> x0, waiting for transfers between devices: 105 us -> none  [by_section(): lax.ppermute(flow, 'col', [(at, 2 * (at % pairs) + at // pairs) for at in...]
    all_gather x1, waiting for transfers between devices: 83.5 us -> 0.01 us  [by_section(): flow = lax.all_gather(flow, 'col', axis_index_groups=groups)]
    ppermute x1 -> x0, starting transfers between devices: 4.33 us -> none  [by_section(): lax.ppermute(flow, 'col', [(at, 2 * (at % pairs) + at // pairs) for at in...]
  transfers between devices with their start and end apart: 6 -> 5, of which waited for: 4 -> 3; matrix products, arithmetic and copies ran while one was open for 8% -> 9% of each run, Pallas kernels for 0% -> 0%
where the time goes in v2:
time: 384 us; the launch traced here: 378 us
  waiting for transfers between devices  260 us (68%)
  Pallas kernels  38.9 us (10%)
  local copies, waits for them, and re-layouts  25.4 us (7%)
  matrix products  20.5 us (5%)
  between operations  14.2 us (4%)
  starting transfers between devices  12.5 us (3%)
  other arithmetic  6.79 us (2%)
    all_to_all x1, waiting for transfers between devices, by_section(): lines = lax.all_to_all(sent, axes, 0, 0, tiled=True).reshape(total, modes)  168 us
    all_to_all x1, waiting for transfers between devices, by_section(): lax.all_to_all(forcing.reshape(device_count, local_waves, modes), axes, 0...  89.3 us
    pallas_call x1, Pallas kernels, advance_waves(): pl.pallas_call(functools.partial(section_kernel, total), grid=(blocks,),...  38.9 us
    dot_general x2, matrix products, to_levels(): return jnp.einsum('pj,zj->pz', lines, table, precision=high)  14.6 us
  transfers between devices with their start and end apart: 5, of which 3 were waited for; matrix products, arithmetic and copies ran while one was open for 9% of the time, Pallas kernels for 0%

profile of v2, /device:TPU:15, one launch (start us, length us, event | category | flops | bytes accessed | tf_op | source)
XLA Modules:
  0.0 378.3 jit_solution(11193004421871959626)
XLA Ops:
  6.5 4.9 %copy.43 = f32[2,2,8,64,512]{4,3,1,2,0:T(8,128)} copy(f32[2,2,8,64,512]{4,3,2,1,0:T(8,128)} %param.14) | data formatting | bytes 8388608 | tf_op args[0]
  11.5 6.3 %all-to-all-start = ((f32[32,64,512]{2,1,0:T(8,128)}), f32[32,64,512]{2,1,0:T(8,128)}, u32[]{:S(2)}, u32[]{:S(2)}) async-start(f32[32,64,512]{2,1,0:T(8,128)} %bitcast.38), calls=%async_computation | async-start | bytes 8388608 | tf_op jit(solution)/shard_map/all_to_all | solution.py:391
  17.8 0.0 all-gather.3.cloned.1.call-start
  17.9 0.1 copy.47
  17.9 0.9 select_maximum_fusion
  18.9 0.0 all-gather.3.cloned.1.call-update
  19.0 1.4 constant_dynamic-slice_fusion.2
  20.4 167.9 %all-to-all-done = f32[32,64,512]{2,1,0:T(8,128)} async-done(((f32[32,64,512]{2,1,0:T(8,128)}), f32[32,64,512]{2,1,0:T(8,128)}, u32[]{:S(2)}, u32[]{:S(2)}) %all-to-all-start) | async-done | bytes 4194336 | tf_op jit(solution)/shard_map/all_to_all | solution.py:391
  188.4 7.4 %convolution_bitcast_fusion = f32[2048,512]{1,0:T(8,128)} fusion(f32[2048,512]{1,0:T(8,128)} %bitcast.8, f32[256,512]{1,0:T(8,128)S(1)} %bitcast.44, f32[256,512]{1,0:T(8,128)S(1)} %bitcast.45), kind=kOutput, calls=%fused_computation.2 | convolution fusion | flops 3221487616 | bytes 9437184 | tf_op jit(solution)/shard_map/pj,zj->pz/dot_general | solution.py:402
  195.7 0.5 collective-permute-start
  196.3 0.6 dynamic_slice.26.span_ref
  196.9 0.6 pad_add_fusion.which_ref
  197.5 7.3 %convolution_bitcast_fusion.1.value_own.slope_own = f32[2048,512]{1,0:T(8,128)} fusion(f32[2048,512]{1,0:T(8,128)} %bitcast.8, f32[256,512]{1,0:T(8,128)S(1)} %bitcast.42, f32[256,512]{1,0:T(8,128)S(1)} %bitcast.43), kind=kOutput, calls=%fused_computation.3 | convolution fusion | flops 3221487616 | bytes 9437184 | tf_op jit(solution)/shard_map/pj,zj->pz/dot_general | solution.py:402
  204.8 6.2 %copy.40 = f32[3,2176,8,32]{1,3,2,0:T(8,128)} copy(f32[3,2176,8,32]{1,3,0,2:T(8,128)} %bitcast.40) | data formatting | bytes 13369344 | tf_op jit(solution)/shard_map/transpose | solution.py:388
  211.0 7.5 %copy.41.flow_ref = f32[3,2176,256]{2,1,0:T(8,128)} copy(f32[3,2176,256]{1,2,0:T(8,128)} %bitcast.36) | data formatting | bytes 13369344 | tf_op jit(solution)/shard_map/reshape | solution.py:388
  218.5 0.0 collective-permute-done.value_other.slope_other
  218.5 38.9 %shard_map.136 = (f32[2048,256]{1,0:T(8,128)}, f32[2048,256]{1,0:T(8,128)}) custom-call(s32[2]{0:T(128)} %pad_add_fusion.which_ref, f32[1]{0:T(128)} %dynamic_slice.26.span_ref, f32[2048,512]{1,0:T(8,128)} %convolution_bitcast_fusion.1.value_own.slope_own, f32[2048,512]{1,0:T(8,128)} %collective-permute-done.value_other.slope_other, ...), custom_call_target="tpu_custom_call" | custom-call | tf_op jit(solution)/shard_map/pallas_call | solution.py:331
  257.3 0.0 collective-permute-start.1
  257.3 1.6 copy.42
  258.9 0.1 constant_dynamic-slice_fusion.1
  259.0 2.7 collective-permute-done.1
  261.7 1.9 fusion.11
  263.6 4.0 %convolution_add_fusion = f32[2048,512]{1,0:T(8,128)} fusion(f32[2048,512]{1,0:T(8,128)S(1)} %fusion.11, f32[2048,256]{1,0:T(8,128)S(1)} %copy-done.1, f32[512,256]{0,1:T(8,128)S(1)} %bitcast.47), kind=kOutput, calls=%fused_computation.1 | convolution fusion | flops 1611661312 | bytes 11010048 | tf_op jit(solution)/shard_map/pz,jz->pj/dot_general | solution.py:411
  267.6 5.6 %all-to-all-start.1 = ((f32[32,64,512]{2,1,0:T(8,128)}), f32[32,64,512]{2,1,0:T(8,128)}, u32[]{:S(2)}, u32[]{:S(2)}) async-start(f32[32,64,512]{2,1,0:T(8,128)} %bitcast.39), calls=%async_computation.1 | async-start | bytes 8388608 | tf_op jit(solution)/shard_map/all_to_all | solution.py:414
  273.9 0.1 broadcast_add_fusion.1
  273.9 0.2 broadcast_add_fusion
  274.1 0.3 multiply_add_fusion
  274.5 89.3 %all-to-all-done.1 = f32[32,64,512]{2,1,0:T(8,128)} async-done(((f32[32,64,512]{2,1,0:T(8,128)}), f32[32,64,512]{2,1,0:T(8,128)}, u32[]{:S(2)}, u32[]{:S(2)}) %all-to-all-start.1) | async-done | bytes 4194336 | tf_op jit(solution)/shard_map/all_to_all | solution.py:414
  363.8 3.0 broadcast_multiply_fusion
  366.8 0.4 copy-done
  367.3 1.6 subtract_divide_fusion
  368.9 2.6 copy.44
  (18 shorter events, 0.0 us)
Async XLA Ops:
  11.4 6.4 %copy-start.5 = (f32[2,32]{1,0:T(2,128)S(1)}, f32[2,32]{1,0:T(2,128)}, u32[]{:S(2)}) copy-start(f32[2,32]{1,0:T(2,128)} %param.20) | copy-start | bytes 772
  11.5 6.5 %copy-start.3 = (f32[3,32,2048]{2,1,0:T(8,128)S(1)}, f32[3,32,2048]{2,1,0:T(8,128)}, u32[]{:S(2)}) copy-start(f32[3,32,2048]{2,1,0:T(8,128)} %param.19) | copy-start | bytes 2359300
  11.5 7.5 %copy-start.2 = (f32[512,512]{1,0:T(8,128)S(1)}, f32[512,512]{1,0:T(8,128)}, u32[]{:S(2)}) copy-start(f32[512,512]{1,0:T(8,128)} %param.16) | copy-start | bytes 3145732
  11.5 176.9 %all-to-all-start = ((f32[32,64,512]{2,1,0:T(8,128)}), f32[32,64,512]{2,1,0:T(8,128)}, u32[]{:S(2)}, u32[]{:S(2)}) async-start(f32[32,64,512]{2,1,0:T(8,128)} %bitcast.38), calls=%async_computation | async-start | bytes 8388608 | tf_op jit(solution)/shard_map/all_to_all | solution.py:391
  17.8 187.0 %all-gather.3.cloned.1.call-start = ((), (), s32[]{:S(2)}) async-start(), calls=%async_computation.2 | async-start | bytes 7520256 | tf_op jit(solution)/shard_map/all_gather | solution.py:387
  188.4 7.9 %copy-start.7 = (f32[8]{0:T(128)S(1)}, f32[8]{0:T(128)}, u32[]{:S(2)}) copy-start(f32[8]{0:T(128)} %param.21) | copy-start | bytes 100
  195.7 22.7 %collective-permute-start = (f32[2048,512]{1,0:T(8,128)}, f32[2048,512]{1,0:T(8,128)}, u32[]{:S(2)}, u32[]{:S(2)}) collective-permute-start(f32[2048,512]{1,0:T(8,128)} %convolution_bitcast_fusion), channel_id=1, source_target_pairs={{0,1},{1,0},{2,3},{3,2},{4,5},{5,4},{6,7},{7,6},{8,9},{9,8},{10,11... | collective-permute-start | bytes 12582920 | tf_op jit(solution)/shard_map/ppermute | solution.py:404
  257.3 4.4 %collective-permute-start.1 = (f32[2048,256]{1,0:T(8,128)}, f32[2048,256]{1,0:T(8,128)S(1)}, u32[]{:S(2)}, u32[]{:S(2)}) collective-permute-start(f32[2048,256]{1,0:T(8,128)} %get-tuple-element.8), channel_id=1, source_target_pairs={{0,1},{1,0},{2,3},{3,2},{4,5},{5,4},{6,7},{7,6},{8,9},{9,8},{10,11... | collective-permute-start | bytes 6291464 | tf_op jit(solution)/shard_map/ppermute | solution.py:410
  258.9 4.7 %copy-start.1 = (f32[2048,256]{1,0:T(8,128)S(1)}, f32[2048,256]{1,0:T(8,128)}, u32[]{:S(2)}) copy-start(f32[2048,256]{1,0:T(8,128)} %get-tuple-element.7) | copy-start | bytes 6291460
  267.6 6.2 %copy-start.4 = (f32[512]{0:T(512)S(1)}, f32[512]{0:T(512)}, u32[]{:S(2)}) copy-start(f32[512]{0:T(512)} %param.18) | copy-start | bytes 6148
  267.6 6.5 %copy-start.6 = (f32[2]{0:T(128)S(1)}, f32[2]{0:T(128)}, u32[]{:S(2)}) copy-start(f32[2]{0:T(128)} %param.22) | copy-start | bytes 28
  267.6 96.2 %all-to-all-start.1 = ((f32[32,64,512]{2,1,0:T(8,128)}), f32[32,64,512]{2,1,0:T(8,128)}, u32[]{:S(2)}, u32[]{:S(2)}) async-start(f32[32,64,512]{2,1,0:T(8,128)} %bitcast.39), calls=%async_computation.1 | async-start | bytes 8388608 | tf_op jit(solution)/shard_map/all_to_all | solution.py:414
  363.8 3.4 copy-start
Sparse Core Ops, SparseCore 0:
  20.8 168.1 all-gather.2

commit v3 on v2

--- a/solution.py
+++ b/solution.py
@@ -383,9 +383,13 @@
         jnp.transpose(gradient)[None], ((0, 2), (0, 0), (0, lane_width - scalars))
     )
     flow = jnp.concatenate([velocity, marks], 2)
-    groups = [list(range(0, col_count, 2)), list(range(1, col_count, 2))]
-    flow = lax.all_gather(flow, "col", axis_index_groups=groups)
-    flow = jnp.transpose(flow, (1, 3, 0, 2)).reshape(3, total + lane_width, pairs * level_rows)
+    row_count = lax.axis_size("row")
+    share = level_rows // row_count
+    flow = lax.dynamic_slice_in_dim(flow, lax.axis_index("row") * share, share, 1)
+    groups = [list(range(0, device_count, 2)), list(range(1, device_count, 2))]
+    flow = lax.all_gather(flow, axes, axis_index_groups=groups)
+    flow = flow.reshape(row_count, pairs, 3, share, total + lane_width)
+    flow = jnp.transpose(flow, (2, 4, 1, 0, 3)).reshape(3, total + lane_width, half)
 
     sent = jnp.swapaxes(coefficients, 1, 2).reshape(device_count, local_waves, modes)
     lines = lax.all_to_all(sent, axes, 0, 0, tiled=True).reshape(total, modes)

time: 384 us -> 366 us (0.953)
  waiting for transfers between devices: 260 us -> 239 us
    all_to_all x1, waiting for transfers between devices: 168 us -> 147 us  [by_section(): lines = lax.all_to_all(sent, axes, 0, 0, tiled=True).reshape(total, modes)]
  transfers between devices with their start and end apart: 5 -> 5, of which waited for: 3 -> 3; matrix products, arithmetic and copies ran while one was open for 9% -> 10% of each run, Pallas kernels for 0% -> 0%
where the time goes in v3:
time: 366 us; the launch traced here: 360 us
  waiting for transfers between devices  239 us (65%)
  Pallas kernels  38.9 us (11%)
  local copies, waits for them, and re-layouts  25.8 us (7%)
  matrix products  20.5 us (6%)
  starting transfers between devices  14.9 us (4%)
  between operations  14.2 us (4%)
  other arithmetic  6.63 us (2%)
    all_to_all x1, waiting for transfers between devices, by_section(): lines = lax.all_to_all(sent, axes, 0, 0, tiled=True).reshape(total, modes)  147 us
    all_to_all x1, waiting for transfers between devices, by_section(): lax.all_to_all(forcing.reshape(device_count, local_waves, modes), axes, 0...  89.3 us
    pallas_call x1, Pallas kernels, advance_waves(): pl.pallas_call(functools.partial(section_kernel, total), grid=(blocks,),...  38.9 us
    dot_general x2, matrix products, to_levels(): return jnp.einsum('pj,zj->pz', lines, table, precision=high)  14.7 us
    all_to_all x1, starting transfers between devices, by_section(): lax.all_to_all(forcing.reshape(device_count, local_waves, modes), axes, 0...  7.96 us
    reshape x1, local copies, waits for them, and re-layouts, by_section(): jnp.transpose(flow, (2, 4, 1, 0, 3)).reshape(3, total + lane_width, half)  7.47 us
  transfers between devices with their start and end apart: 5, of which 3 were waited for; matrix products, arithmetic and copies ran while one was open for 10% of the time, Pallas kernels for 0%

profile of v3, /device:TPU:15, one launch (start us, length us, event | category | flops | bytes accessed | tf_op | source)
XLA Modules:
  0.0 360.2 jit_solution(3817524389426213448)
XLA Ops:
  6.5 4.9 %copy.43 = f32[2,2,8,64,512]{4,3,1,2,0:T(8,128)} copy(f32[2,2,8,64,512]{4,3,2,1,0:T(8,128)} %param.14) | data formatting | bytes 8388608 | tf_op args[0]
  11.5 6.3 %all-to-all-start = ((f32[32,64,512]{2,1,0:T(8,128)}), f32[32,64,512]{2,1,0:T(8,128)}, u32[]{:S(2)}, u32[]{:S(2)}) async-start(f32[32,64,512]{2,1,0:T(8,128)} %bitcast.38), calls=%async_computation | async-start | bytes 8388608 | tf_op jit(solution)/shard_map/all_to_all | solution.py:395
  17.8 0.0 all-gather.3.cloned.1.call-start
  17.9 0.1 copy.47
  17.9 0.8 fusion.6
  18.7 0.0 all-gather.3.cloned.1.call-update
  18.8 1.4 constant_dynamic-slice_fusion.2
  20.3 147.3 %all-to-all-done = f32[32,64,512]{2,1,0:T(8,128)} async-done(((f32[32,64,512]{2,1,0:T(8,128)}), f32[32,64,512]{2,1,0:T(8,128)}, u32[]{:S(2)}, u32[]{:S(2)}) %all-to-all-start) | async-done | bytes 4194336 | tf_op jit(solution)/shard_map/all_to_all | solution.py:395
  167.6 7.4 %convolution_bitcast_fusion = f32[2048,512]{1,0:T(8,128)} fusion(f32[2048,512]{1,0:T(8,128)} %bitcast.8, f32[256,512]{1,0:T(8,128)S(1)} %bitcast.44, f32[256,512]{1,0:T(8,128)S(1)} %bitcast.45), kind=kOutput, calls=%fused_computation.2 | convolution fusion | flops 3221487616 | bytes 9437184 | tf_op jit(solution)/shard_map/pj,zj->pz/dot_general | solution.py:406
  174.9 0.5 collective-permute-start
  175.5 0.6 dynamic_slice.29.span_ref
  176.1 0.6 pad_add_fusion.which_ref
  176.7 7.3 %convolution_bitcast_fusion.1.value_own.slope_own = f32[2048,512]{1,0:T(8,128)} fusion(f32[2048,512]{1,0:T(8,128)} %bitcast.8, f32[256,512]{1,0:T(8,128)S(1)} %bitcast.42, f32[256,512]{1,0:T(8,128)S(1)} %bitcast.43), kind=kOutput, calls=%fused_computation.3 | convolution fusion | flops 3221487616 | bytes 9437184 | tf_op jit(solution)/shard_map/pj,zj->pz/dot_general | solution.py:406
  184.0 6.6 %copy.40 = f32[3,2176,8,2,16]{1,4,3,2,0:T(8,128)} copy(f32[3,2176,8,2,16]{1,4,0,2,3:T(8,128)} %bitcast.40) | data formatting | bytes 13369344 | tf_op jit(solution)/shard_map/transpose | solution.py:392
  190.5 7.5 %copy.41.flow_ref = f32[3,2176,256]{2,1,0:T(8,128)} copy(f32[3,2176,256]{1,2,0:T(8,128)} %bitcast.36) | data formatting | bytes 13369344 | tf_op jit(solution)/shard_map/reshape | solution.py:392
  198.0 0.0 collective-permute-done.value_other.slope_other
  198.0 38.9 %shard_map.136 = (f32[2048,256]{1,0:T(8,128)}, f32[2048,256]{1,0:T(8,128)}) custom-call(s32[2]{0:T(128)} %pad_add_fusion.which_ref, f32[1]{0:T(128)} %dynamic_slice.29.span_ref, f32[2048,512]{1,0:T(8,128)} %convolution_bitcast_fusion.1.value_own.slope_own, f32[2048,512]{1,0:T(8,128)} %collective-permute-done.value_other.slope_other, ...), custom_call_target="tpu_custom_call" | custom-call | tf_op jit(solution)/shard_map/pallas_call | solution.py:331
  236.9 0.0 collective-permute-start.1
  236.9 1.6 copy.42
  238.5 0.1 constant_dynamic-slice_fusion.1
  238.5 2.7 collective-permute-done.1
  241.2 1.9 fusion.13
  243.1 4.0 %convolution_add_fusion = f32[2048,512]{1,0:T(8,128)} fusion(f32[2048,512]{1,0:T(8,128)S(1)} %fusion.13, f32[2048,256]{1,0:T(8,128)S(1)} %copy-done.1, f32[512,256]{0,1:T(8,128)S(1)} %bitcast.47), kind=kOutput, calls=%fused_computation.1 | convolution fusion | flops 1611661312 | bytes 11010048 | tf_op jit(solution)/shard_map/pz,jz->pj/dot_general | solution.py:415
  247.1 8.0 %all-to-all-start.1 = ((f32[32,64,512]{2,1,0:T(8,128)}), f32[32,64,512]{2,1,0:T(8,128)}, u32[]{:S(2)}, u32[]{:S(2)}) async-start(f32[32,64,512]{2,1,0:T(8,128)} %bitcast.39), calls=%async_computation.1 | async-start | bytes 8388608 | tf_op jit(solution)/shard_map/all_to_all | solution.py:418
  255.8 0.1 broadcast_add_fusion.1
  255.9 0.2 broadcast_add_fusion
  256.1 0.3 multiply_add_fusion
  256.4 89.3 %all-to-all-done.1 = f32[32,64,512]{2,1,0:T(8,128)} async-done(((f32[32,64,512]{2,1,0:T(8,128)}), f32[32,64,512]{2,1,0:T(8,128)}, u32[]{:S(2)}, u32[]{:S(2)}) %all-to-all-start.1) | async-done | bytes 4194336 | tf_op jit(solution)/shard_map/all_to_all | solution.py:418
  345.7 3.0 broadcast_multiply_fusion
  348.7 0.4 copy-done
  349.2 1.6 subtract_divide_fusion
  350.8 2.6 copy.44
  (18 shorter events, 0.0 us)
Async XLA Ops:
  11.4 6.4 %copy-start.5 = (f32[2,32]{1,0:T(2,128)S(1)}, f32[2,32]{1,0:T(2,128)}, u32[]{:S(2)}) copy-start(f32[2,32]{1,0:T(2,128)} %param.20) | copy-start | bytes 772
  11.5 6.5 %copy-start.3 = (f32[3,32,2048]{2,1,0:T(8,128)S(1)}, f32[3,32,2048]{2,1,0:T(8,128)}, u32[]{:S(2)}) copy-start(f32[3,32,2048]{2,1,0:T(8,128)} %param.19) | copy-start | bytes 2359300
  11.5 7.3 %copy-start.2 = (f32[512,512]{1,0:T(8,128)S(1)}, f32[512,512]{1,0:T(8,128)}, u32[]{:S(2)}) copy-start(f32[512,512]{1,0:T(8,128)} %param.16) | copy-start | bytes 3145732
  11.5 156.1 %all-to-all-start = ((f32[32,64,512]{2,1,0:T(8,128)}), f32[32,64,512]{2,1,0:T(8,128)}, u32[]{:S(2)}, u32[]{:S(2)}) async-start(f32[32,64,512]{2,1,0:T(8,128)} %bitcast.38), calls=%async_computation | async-start | bytes 8388608 | tf_op jit(solution)/shard_map/all_to_all | solution.py:395
  17.8 166.2 %all-gather.3.cloned.1.call-start = ((), (), s32[]{:S(2)}) async-start(), calls=%async_computation.2 | async-start | bytes 7102464 | tf_op jit(solution)/shard_map/all_gather | solution.py:390
  167.6 7.9 %copy-start.7 = (f32[8]{0:T(128)S(1)}, f32[8]{0:T(128)}, u32[]{:S(2)}) copy-start(f32[8]{0:T(128)} %param.21) | copy-start | bytes 100
  174.9 23.1 %collective-permute-start = (f32[2048,512]{1,0:T(8,128)}, f32[2048,512]{1,0:T(8,128)}, u32[]{:S(2)}, u32[]{:S(2)}) collective-permute-start(f32[2048,512]{1,0:T(8,128)} %convolution_bitcast_fusion), channel_id=1, source_target_pairs={{0,1},{1,0},{2,3},{3,2},{4,5},{5,4},{6,7},{7,6},{8,9},{9,8},{10,11... | collective-permute-start | bytes 12582920 | tf_op jit(solution)/shard_map/ppermute | solution.py:408
  236.9 4.4 %collective-permute-start.1 = (f32[2048,256]{1,0:T(8,128)}, f32[2048,256]{1,0:T(8,128)S(1)}, u32[]{:S(2)}, u32[]{:S(2)}) collective-permute-start(f32[2048,256]{1,0:T(8,128)} %get-tuple-element.8), channel_id=1, source_target_pairs={{0,1},{1,0},{2,3},{3,2},{4,5},{5,4},{6,7},{7,6},{8,9},{9,8},{10,11... | collective-permute-start | bytes 6291464 | tf_op jit(solution)/shard_map/ppermute | solution.py:414
  238.4 4.7 %copy-start.1 = (f32[2048,256]{1,0:T(8,128)S(1)}, f32[2048,256]{1,0:T(8,128)}, u32[]{:S(2)}) copy-start(f32[2048,256]{1,0:T(8,128)} %get-tuple-element.7) | copy-start | bytes 6291460
  247.1 8.7 %copy-start.4 = (f32[512]{0:T(512)S(1)}, f32[512]{0:T(512)}, u32[]{:S(2)}) copy-start(f32[512]{0:T(512)} %param.18) | copy-start | bytes 6148
  247.1 8.9 %copy-start.6 = (f32[2]{0:T(128)S(1)}, f32[2]{0:T(128)}, u32[]{:S(2)}) copy-start(f32[2]{0:T(128)} %param.22) | copy-start | bytes 28
  247.1 98.6 %all-to-all-start.1 = ((f32[32,64,512]{2,1,0:T(8,128)}), f32[32,64,512]{2,1,0:T(8,128)}, u32[]{:S(2)}, u32[]{:S(2)}) async-start(f32[32,64,512]{2,1,0:T(8,128)} %bitcast.39), calls=%async_computation.1 | async-start | bytes 8388608 | tf_op jit(solution)/shard_map/all_to_all | solution.py:418
  345.7 3.4 copy-start
Sparse Core Ops, SparseCore 0:
  21.4 149.6 all-gather.2
